TPU v7x, 256 devices: a whole 4x4x8 slice. The times are simulated.
256 devices in a mesh: dp: 32 (over y, x, core), tensor: 8 (over z).
Axes of the slice: x: 4, y: 4, z: 8, core: 2. Of those that a mesh axis runs over, the one named last changes fastest.
Arguments:
- acts: bfloat16 [16384, 8192], P('dp', 'tensor'), may hold values from -6 to 6
- weight: bfloat16 [8192, 5120], P('tensor'), may hold values from -0.09375 to 0.09375
- block_ids: int32 [128], P('dp'), may hold values from 0 to 511
- cached_a: bfloat16 [128, 8192, 64], P('dp', 'tensor'), may hold values from -0.0625 to 0.0625
- cached_b: bfloat16 [128, 64, 5120], P('dp', None, 'tensor'), may hold values from -0.75 to 0.75
- renewed_module_numbers: int32 [64], replicated, may hold values from 0 to 511, as said below
- fresh_a: bfloat16 [64, 8192, 64], P('dp', 'tensor'), may hold values from -0.0625 to 0.0625
- renewed_second_matrices: bfloat16 [64, 64, 5120], P('dp', None, 'tensor'), may hold values from -0.75 to 0.75
Outputs:
- projected: bfloat16 [16384, 5120], P('dp', 'tensor')
Inputs may be any that keep to these rules, and one draw needn't show every extreme that they name: `renewed_module_numbers`: the ids are distinct, and each is the id of at least one block.
All inputs are finite; a program needn't handle non-finite values.
Results may differ from a plain program's by a relative error of at most 0.0095.
Values may be sent and summed in bfloat16 or wider, within the bound.
A program may use at most 128 MiB of HBM per device.

v0:
```python
import jax
import jax.numpy as jnp
from jax import lax
from jax.sharding import PartitionSpec as P

adapter_scale = 2.0


def expand_rows(shrink, adapter_factor):
    upper_portion = shrink.astype(jnp.bfloat16)
    lower_portion = (shrink - upper_portion.astype(jnp.float32)).astype(jnp.bfloat16)
    upper_bound_index = jnp.einsum(
        "aul,alf->auf", upper_portion, adapter_factor, preferred_element_type=jnp.float32
    )
    lower_bound_index = jnp.einsum(
        "aul,alf->auf", lower_portion, adapter_factor, preferred_element_type=jnp.float32
    )
    return upper_bound_index + lower_bound_index


def shards(
    acts,
    weight,
    block_ids,
    cached_a,
    cached_b,
    renewed_module_numbers,
    fresh_a,
    renewed_second_matrices,
):
    blocks_here = block_ids.shape[0]
    rows_here = acts.shape[0]
    block_rows = rows_here // blocks_here
    matches = block_ids[:, None] == renewed_module_numbers[None, :]
    refreshed = jnp.any(matches, axis=1)[:, None, None]
    every_a, widening_matrices = (
        lax.all_gather(fresh_a, "dp", axis=0, tiled=True),
        lax.all_gather(renewed_second_matrices, "dp", axis=0, tiled=True),
    )
    module_picker_matrix = matches.astype(jnp.bfloat16)
    chosen_narrowing_matrix = jnp.einsum(
        "bj,jik->bik", module_picker_matrix, every_a, preferred_element_type=jnp.float32
    )
    selected_up_factor = jnp.einsum(
        "pk,kyz->pyz", module_picker_matrix, widening_matrices, preferred_element_type=jnp.float32
    )
    narrowing_matrix = jnp.where(refreshed, chosen_narrowing_matrix.astype(jnp.bfloat16), cached_a)
    factor_b = jnp.where(refreshed, selected_up_factor.astype(jnp.bfloat16), cached_b)
    grouped = acts.reshape(blocks_here, block_rows, acts.shape[1])
    partial_value = jnp.einsum(
        "bri,bik->brk", grouped, narrowing_matrix, preferred_element_type=jnp.float32
    )
    base_product_sum = jnp.dot(acts, weight, preferred_element_type=jnp.float32)
    shrink = lax.psum(partial_value, "tensor")
    expand_factor_up = expand_rows(shrink, factor_b).reshape(rows_here, factor_b.shape[2])
    reduced_output = lax.psum_scatter(base_product_sum, "tensor", scatter_dimension=1, tiled=True)
    return (reduced_output + adapter_scale * expand_factor_up).astype(jnp.bfloat16)


def solution(mesh):
    return jax.shard_map(
        shards,
        mesh=mesh,
        in_specs=(
            P("dp", "tensor"),
            P("tensor", None),
            P("dp"),
            P("dp", "tensor", None),
            P("dp", None, "tensor"),
            P(),
            P("dp", "tensor", None),
            P("dp", None, "tensor"),
        ),
        out_specs=P("dp", "tensor"),
        check_vma=False,
    )
```

profile of v0, /device:TPU:4, one launch (start us, length us, event | category | flops | bytes accessed | tf_op | source)
XLA Modules:
  0.0 323.8 jit_solution(15388350129072115105)
XLA Ops:
  6.5 0.0 copy-start
  6.5 0.0 all-gather.3.cloned.1.call-start
  6.5 0.7 all-gather.3.cloned.1.call-update
  7.3 0.0 all-gather.5.cloned.1.call-start
  7.3 0.7 all-gather.5.cloned.1.call-update
  8.0 0.0 all-reduce.2.cloned.1.call-start
  8.1 0.9 compare_reduce_fusion
  8.9 61.9 %all-gather.3.cloned.1.call-done = bf16[64,1024,64]{1,2,0:T(8,128)(2,1)} async-done(((bf16[2,1024,64]{1,2,0:T(8,128)(2,1)}), bf16[64,1024,64]{1,2,0:T(8,128)(2,1)}) %all-gather.3.cloned.1.call-update) | async-done | bytes 8388624 | tf_op jit(solution)/shard_map/all_gather | solution.py:37
  70.8 12.3 %fusion = bf16[4,1024,64]{1,0,2:T(4,128)(2,1)S(1)} fusion(bf16[64,1024,64]{1,2,0:T(8,128)(2,1)} %all-gather.3.cloned.1.call-done, s32[64]{0:T(128)} %param.13, s32[4]{0:T(128)} %param.10), kind=kOutput, calls=%fused_computation | convolution fusion | flops 33554688 | bytes 8913168 | tf_op jit(solution)/shard_map/bj,jik->bik/dot_general | solution.py:41
  83.1 0.0 copy-done
  83.1 0.0 copy-done.3
  83.1 1.2 convolution_bitcast_fusion
  84.3 0.0 all-reduce.2.cloned.1.call-update
  84.4 0.2 reduce-scatter.2.cloned.1.call-start
  84.6 12.2 %fusion.20 = f32[512,5120]{1,0:T(8,128)} fusion(bf16[512,1024]{1,0:T(8,128)(2,1)S(1)} %copy-done, bf16[1024,5120]{1,0:T(8,128)(2,1)} %param.9), kind=kOutput, calls=%fused_computation.22 | convolution fusion | flops 5368709120 | bytes 22020096 | tf_op jit(solution)/shard_map/dot_general | solution.py:53
  96.8 0.0 reduce-scatter.2.cloned.1.call-update
  96.9 27.5 %all-gather.5.cloned.1.call-done = bf16[64,64,640]{2,1,0:T(8,128)(2,1)} async-done(((bf16[2,64,640]{2,1,0:T(8,128)(2,1)}), bf16[64,64,640]{2,1,0:T(8,128)(2,1)}) %all-gather.5.cloned.1.call-update) | async-done | bytes 5242896 | tf_op jit(solution)/shard_map/all_gather | solution.py:38
  124.4 0.0 copy-done.1
  124.4 8.1 %fusion.9 = bf16[4,64,640]{2,0,1:T(4,128)(2,1)S(1)} fusion(bf16[64,64,640]{2,1,0:T(8,128)(2,1)} %all-gather.5.cloned.1.call-done, bf16[4,64,640]{2,1,0:T(8,128)(2,1)S(1)} %copy-done.4, pred[4]{0:T(512)(128)(4,1)S(1)} %compare_reduce_fusion, s32[64]{0:T(128)S(1)} %copy-done.1, s32[4]{0:T(128)S(1)} %copy-done.2), kind=kOutput, calls=%fused_computation.11 | convolution fusion | flops 21299456 | bytes 5898516 | tf_op jit(solution)/shard_map/pk,kyz->pyz/dot_general | solution.py:44
  132.5 66.6 %all-reduce.2.cloned.1.call-done = f32[4,128,64]{1,2,0:T(8,128)} async-done(((f32[4,128,64]{1,2,0:T(8,128)}), f32[4,128,64]{1,2,0:T(8,128)}) %all-reduce.2.cloned.1.call-update) | async-done | bytes 131088 | tf_op jit(solution)/shard_map/psum | solution.py:54
  199.1 1.3 fusion.16
  200.4 1.4 fusion.4
  201.8 113.1 %reduce-scatter.2.cloned.1.call-done = f32[512,640]{1,0:T(8,128)} async-done(((f32[512,5120]{1,0:T(8,128)}), f32[512,640]{1,0:T(8,128)}) %reduce-scatter.2.cloned.1.call-update) | async-done | bytes 1310736 | tf_op jit(solution)/shard_map/reduce_scatter | solution.py:56
  314.9 2.3 fusion.5
  (6 shorter events, 0.0 us)
Async XLA Ops:
  6.5 76.6 %copy-start = (bf16[512,1024]{1,0:T(8,128)(2,1)S(1)}, bf16[512,1024]{1,0:T(8,128)(2,1)}, u32[]{:S(2)}) copy-start(bf16[512,1024]{1,0:T(8,128)(2,1)} %param.8) | copy-start | bytes 3145732
  6.5 76.6 %copy-start.3 = (bf16[4,1024,64]{1,2,0:T(8,128)(2,1)S(1)}, bf16[4,1024,64]{1,2,0:T(8,128)(2,1)}, u32[]{:S(2)}) copy-start(bf16[4,1024,64]{1,2,0:T(8,128)(2,1)} %param.11) | copy-start | bytes 1572868
  6.5 64.2 %all-gather.3.cloned.1.call-start = ((), (), s32[]{:S(2)}) async-start(), calls=%async_computation.2 | async-start | bytes 8650752 | tf_op jit(solution)/shard_map/all_gather | solution.py:37
  7.3 117.1 %all-gather.5.cloned.1.call-start = ((), (), s32[]{:S(2)}) async-start(), calls=%async_computation.4 | async-start | bytes 5406720 | tf_op jit(solution)/shard_map/all_gather | solution.py:38
  8.0 191.1 %all-reduce.2.cloned.1.call-start = ((), (), s32[]{:S(2)}) async-start(), calls=%async_computation.3 | async-start | bytes 262144 | tf_op jit(solution)/shard_map/psum | solution.py:54
  84.4 230.5 %reduce-scatter.2.cloned.1.call-start = ((), (), s32[]{:S(2)}) async-start(), calls=%async_computation.1 | async-start | bytes 11796480 | tf_op jit(solution)/shard_map/reduce_scatter | solution.py:56
  96.8 27.6 %copy-start.1 = (s32[64]{0:T(128)S(1)}, s32[64]{0:T(128)}, u32[]{:S(2)}) copy-start(s32[64]{0:T(128)} %param.13) | copy-start | bytes 772
  96.8 27.6 %copy-start.2 = (s32[4]{0:T(128)S(1)}, s32[4]{0:T(128)}, u32[]{:S(2)}) copy-start(s32[4]{0:T(128)} %param.10) | copy-start | bytes 52
  96.8 27.6 %copy-start.4 = (bf16[4,64,640]{2,1,0:T(8,128)(2,1)S(1)}, bf16[4,64,640]{2,1,0:T(8,128)(2,1)}, u32[]{:S(2)}) copy-start(bf16[4,64,640]{2,1,0:T(8,128)(2,1)} %param.12) | copy-start | bytes 983044
Sparse Core Ops, SparseCore 0:
  9.9 60.8 all-gather.2
  73.3 51.0 all-gather.4
  126.7 72.3 all-reduce.1
  201.7 113.1 reduce-scatter.1
where the time goes:
time: 325 us; the launch traced here: 324 us
  waiting for transfers between devices  271 us (83%)
  matrix products  36.5 us (11%)
  between operations  13.1 us (4%)
    reduce_scatter x1, waiting for transfers between devices, shards(): lax.psum_scatter(base_product_sum, 'tensor', scatter_dimension=1, tiled=T...  113 us
    psum x1, waiting for transfers between devices, shards(): shrink = lax.psum(partial_value, 'tensor')  66.6 us
    all_gather x1, waiting for transfers between devices, shards(): lax.all_gather(fresh_a, 'dp', axis=0, tiled=True)  61.9 us
    all_gather x1, waiting for transfers between devices, shards(): lax.all_gather(renewed_second_matrices, 'dp', axis=0, tiled=True)  27.5 us
    dot_general x1, matrix products, shards(): jnp.einsum('bj,jik->bik', module_picker_matrix, every_a, preferred_elemen...  12.3 us
    dot_general x1, matrix products, shards(): base_product_sum = jnp.dot(acts, weight, preferred_element_type=jnp.float32)  12.2 us
    dot_general x1, matrix products, shards(): jnp.einsum('pk,kyz->pyz', module_picker_matrix, widening_matrices, prefer...  8.1 us
  transfers between devices with their start and end apart: 4, of which 4 were waited for; matrix products, arithmetic and copies ran while one was open for 12% of the time, Pallas kernels for 0%

commit v1 on v0

v1 whole, which is shorter than its diff:
```python
import jax
import jax.numpy as jnp
from jax import lax
from jax.experimental import pallas as pl
from jax.experimental.pallas import tpu as pltpu
from jax.sharding import PartitionSpec as P

adapter_scale = 2.0
Z = 8
SIDE = 4
TILE = 128
BF16 = jnp.bfloat16
F32 = jnp.float32

SLOTS = (
    (True, 0, None),
    (False, 1, None),
    (True, 1, 0),
    (False, 2, 1),
    (True, 2, 2),
    (False, 3, 3),
    (True, 3, 4),
)
LAST_LONG, LAST_SHORT = 6, 5

FIRST, SECOND, FIRST_FAR, SECOND_PAIR, SECOND_FAR, OWN_ON, PAIR_ON, FAR_ON = range(8)
ROWS_ACROSS = 16


def dot(a, b):
    return jnp.dot(a, b, preferred_element_type=F32)


def kernel(
    acts_hbm, weight_hbm, ids_hbm, cached_a_hbm, cached_b_hbm, renewed_hbm, fresh_a_hbm, fresh_b_hbm,
    out_hbm,
    acts, weight, ids, renewed, cached_a, cached_b, every_a, every_b,
    outgoing, incoming, total, result, part_out, part_in, shrunk,
    load_sem, weight_sem, fresh_sem, out_sem,
    ring_send, ring_recv, gather_send, gather_recv, part_send, part_recv, shrunk_send, shrunk_recv,
):
    z = lax.axis_index("tensor")
    dp = lax.axis_index("dp")
    core = dp % 2
    x = (dp // 2) % SIDE
    y = dp // (2 * SIDE)
    depth, width = weight.shape[1], weight.shape[2]
    blocks = ids_hbm.shape[0]
    rows = acts.shape[0]
    half = rows // 2
    tiles = half // TILE
    rank = cached_a.shape[1]

    def at_xy(px, py, pc):
        return {"dp": (py * SIDE + px) * 2 + pc}

    def along(axis, step):
        if axis == 0:
            return at_xy((x + step + SIDE) % SIDE, y, core)
        return at_xy(x, (y + step + SIDE) % SIDE, core)

    sibling = at_xy(x, y, 1 - core)

    def weight_load(i):
        column = pl.multiple_of((z + i) % Z * width, 128)
        return pltpu.make_async_copy(weight_hbm.at[:, pl.ds(column, width)], weight.at[i], weight_sem.at[i])

    loads = [
        pltpu.make_async_copy(acts_hbm, acts, load_sem.at[0]),
        pltpu.make_async_copy(cached_a_hbm, cached_a, load_sem.at[1]),
        pltpu.make_async_copy(cached_b_hbm, cached_b, load_sem.at[2]),
        pltpu.make_async_copy(ids_hbm, ids, load_sem.at[3]),
        pltpu.make_async_copy(renewed_hbm, renewed, load_sem.at[4]),
    ]
    mine = (
        (core * SIDE + y) * SIDE + (x % 2) * 2 + x // 2,
        ((2 + core) * SIDE + x) * SIDE + (y % 2) * 2 + y // 2,
    )
    gathers = ((every_a, fresh_a_hbm), (every_b, fresh_b_hbm))
    fresh_loads = [
        [pltpu.make_async_copy(source.at[j], held.at[mine[j]], fresh_sem.at[g, j]) for j in range(2)]
        for g, (held, source) in enumerate(gathers)
    ]

    loads[0].start()
    weight_load(4).start()

    barrier = pltpu.get_barrier_semaphore()
    for i in range(1, Z):
        pl.semaphore_signal(barrier, inc=1, device_id={"tensor": (z + i) % Z}, device_id_type=pl.DeviceIdType.MESH)
    for axis in range(2):
        for step in (1, -1):
            pl.semaphore_signal(barrier, inc=1, device_id=along(axis, step), device_id_type=pl.DeviceIdType.MESH)
    pl.semaphore_signal(barrier, inc=1, device_id=sibling, device_id_type=pl.DeviceIdType.MESH)

    for j in range(2):
        fresh_loads[0][j].start()
    for i in (3, 5, 2, 6, 1, 7, 0):
        weight_load(i).start()
    for j in range(2):
        fresh_loads[1][j].start()
    for load in loads[1:]:
        load.start()

    def ring_copy(direction, slot, tile):
        spot = pl.ds(tile * TILE, TILE)
        return pltpu.make_async_remote_copy(
            src_ref=outgoing.at[direction, slot, spot],
            dst_ref=incoming.at[direction, slot, spot],
            send_sem=ring_send.at[direction, slot, tile],
            recv_sem=ring_recv.at[direction, slot, tile],
            device_id={"tensor": (z + 1 - 2 * direction + Z) % Z},
            device_id_type=pl.DeviceIdType.MESH,
        )

    ways = [(direction, tile) for tile in range(tiles) for direction in range(2)]

    def lines(direction, is_long, tile):
        side = direction if is_long else 1 - direction
        return pl.ds(side * half + tile * TILE, TILE)

    def ring_step(slot, send):
        is_long, step, before = SLOTS[slot]
        if is_long and step == 0:
            weight_load(4).wait()
        elif not is_long:
            weight_load(4 - step).wait()
            weight_load(4 + step).wait()
        for direction, tile in ways:
            spot = pl.ds(tile * TILE, TILE)
            term = dot(acts[lines(direction, is_long, tile)], weight[4 - step + 2 * step * direction])
            if before is not None:
                ring_copy(direction, before, tile).wait_recv()
                term = term + incoming[direction, before, spot].astype(F32)
            outgoing[direction, slot, spot] = term.astype(BF16)
            if send:
                ring_copy(direction, slot, tile).start()

    def line_of(j, second, of_core):
        return ((j * 2 + of_core) * SIDE + second) * SIDE

    def across_line(first):
        return (first % 2) * 2 + first // 2

    def gather_copy(g, j, kind, direction=0, incoming_side=False):
        held = gathers[g][0]
        first, second = (x, y) if j == 0 else (y, x)
        first_axis, second_axis = (0, 1) if j == 0 else (1, 0)
        sign = 1 - 2 * direction
        back = -sign if incoming_side else 0
        here = across_line(first)
        pair = (1 - first % 2) * 2
        far = across_line((first + 2) % SIDE)
        part = pl.ds(direction * (rank // 2), rank // 2)

        def line(step):
            return line_of(j, (second + step + SIDE) % SIDE, core)

        axis = second_axis
        if kind == FIRST:
            axis = first_axis
            ref = held.at[line(0) + across_line((first + back + SIDE) % SIDE)]
        elif kind == FIRST_FAR:
            axis = first_axis
            ref = held.at[line(0) + across_line((first + back - sign + SIDE) % SIDE), part]
        elif kind == SECOND:
            ref = held.at[line(back) + here]
        elif kind == SECOND_PAIR:
            ref = held.at[pl.ds(line(back) + pair, 2)]
        elif kind == SECOND_FAR:
            ref = held.at[line(back) + far]
        elif kind == OWN_ON:
            ref = held.at[line(back - sign) + here, part]
        elif kind == PAIR_ON:
            ref = held.at[line(back - sign) + pair + direction]
        else:
            ref = held.at[line(back - sign) + far, part]
        number = 2 * kind + direction
        return pltpu.make_async_remote_copy(
            src_ref=ref, dst_ref=ref,
            send_sem=gather_send.at[g, j, number], recv_sem=gather_recv.at[g, j, number],
            device_id=along(axis, sign), device_id_type=pl.DeviceIdType.MESH,
        )

    def across_copy(g, j, number, incoming_side=False):
        held = gathers[g][0]
        second = y if j == 0 else x
        moved = (second + (0, -1, 1, 2)[number] + SIDE) % SIDE
        ref = held.at[pl.ds(line_of(j, moved, 1 - core if incoming_side else core), SIDE)]
        return pltpu.make_async_remote_copy(
            src_ref=ref, dst_ref=ref,
            send_sem=gather_send.at[g, j, ROWS_ACROSS + number], recv_sem=gather_recv.at[g, j, ROWS_ACROSS + number],
            device_id=sibling, device_id_type=pl.DeviceIdType.MESH,
        )

    both = [(j, direction) for j in range(2) for direction in range(2)]

    def send_all(g, *kinds):
        for kind in kinds:
            for j, direction in both:
                gather_copy(g, j, kind, direction).start()

    def take_all(g, *kinds):
        for kind in kinds:
            for j, direction in both:
                gather_copy(g, j, kind, direction, True).wait_recv()

    def send_across(g, *numbers):
        for number in numbers:
            for j in range(2):
                across_copy(g, j, number).start()

    def gather_0(g):
        for j in range(2):
            fresh_loads[g][j].wait()
        send_all(g, FIRST, SECOND)

    def gather_1(g):
        take_all(g, FIRST)
        send_all(g, FIRST_FAR, SECOND_PAIR)

    def gather_2(g):
        take_all(g, FIRST_FAR)
        send_all(g, SECOND_FAR)
        send_across(g, 0)

    def gather_3(g):
        take_all(g, SECOND)
        send_all(g, OWN_ON)
        take_all(g, SECOND_PAIR)
        send_all(g, PAIR_ON)

    def gather_4(g):
        take_all(g, SECOND_FAR)
        send_all(g, FAR_ON)
        send_across(g, 1, 2)

    def gather_5(g):
        take_all(g, OWN_ON, PAIR_ON, FAR_ON)
        send_across(g, 3)

    def gather_6(g):
        for number in range(4):
            for j in range(2):
                across_copy(g, j, number, True).wait_recv()

    def match(b):
        def body(i, carry):
            found, where = carry
            hit = renewed[i] == ids[b]
            return jnp.where(hit, 1, found), jnp.where(hit, i, where)

        return lax.fori_loop(0, renewed_hbm.shape[0], body, (jnp.int32(0), jnp.int32(0)))

    def chosen(held, cached, b, found, where):
        j, of_core, px, py = where % 2, (where // 2) % 2, (where // 4) % SIDE, where // 16
        second, first = jnp.where(j == 0, py, px), jnp.where(j == 0, px, py)
        return jnp.where(found > 0, held[line_of(j, second, of_core) + across_line(first)], cached[b])

    piece = rows // Z

    def part_copy(i):
        return pltpu.make_async_remote_copy(
            src_ref=part_out.at[(z + i) % Z], dst_ref=part_in.at[i],
            send_sem=part_send.at[i], recv_sem=part_recv.at[i],
            device_id={"tensor": (z + i) % Z}, device_id_type=pl.DeviceIdType.MESH,
        )

    def shrunk_copy(i):
        return pltpu.make_async_remote_copy(
            src_ref=shrunk.at[0], dst_ref=shrunk.at[i],
            send_sem=shrunk_send.at[i], recv_sem=shrunk_recv.at[i],
            device_id={"tensor": (z + i) % Z}, device_id_type=pl.DeviceIdType.MESH,
        )

    def shrink_parts(matches):
        for b in range(blocks):
            factor = chosen(every_a, cached_a, b, *matches[b])
            part = lax.dot_general(
                acts[pl.ds(b * TILE, TILE)], factor, (((1,), (1,)), ((), ())), preferred_element_type=F32
            )
            for q in range(TILE // piece):
                upper = part[q * piece : q * piece + piece // 2]
                lower = part[q * piece + piece // 2 : (q + 1) * piece]
                part_out[b * (TILE // piece) + q] = jnp.concatenate([upper, lower], axis=1).astype(BF16)
        for i in range(1, Z):
            part_copy(i).start()

    def shrink_sum():
        value = part_out[z].astype(F32)
        for i in range(1, Z):
            part_copy(i).wait_recv()
            value = value + part_in[i].astype(F32)
        shrunk[0] = value.astype(BF16)
        for i in range(1, Z):
            shrunk_copy(i).start()

    def expand(matches):
        for i in range(1, Z):
            shrunk_copy(i).wait_recv()
        for b in range(blocks):
            factor = chosen(every_b, cached_b, b, *matches[b])
            lines = []
            for q in range(TILE // piece):
                packed = shrunk[(z + Z - b * (TILE // piece) - q) % Z].astype(F32)
                lines += [packed[:, :rank], packed[:, rank:]]
            lines = jnp.concatenate(lines, axis=0).astype(BF16)
            spot = pl.ds(b * TILE, TILE)
            total[spot] = total[spot] + adapter_scale * dot(lines, factor)

    def own_base():
        weight_load(0).wait()
        for i in range(rows // TILE):
            spot = pl.ds(i * TILE, TILE)
            total[spot] = dot(acts[spot], weight[0])

    def add_short():
        for direction, tile in ways:
            ring_copy(direction, LAST_SHORT, tile).wait_recv()
            spot = lines(direction, False, tile)
            total[spot] = total[spot] + incoming[direction, LAST_SHORT, pl.ds(tile * TILE, TILE)].astype(F32)

    def out_copy(direction, tile):
        spot = lines(direction, True, tile)
        return pltpu.make_async_copy(result.at[spot], out_hbm.at[spot], out_sem.at[direction, tile])

    def finish():
        for direction, tile in ways:
            ring_copy(direction, LAST_LONG, tile).wait_recv()
            spot = lines(direction, True, tile)
            got = incoming[direction, LAST_LONG, pl.ds(tile * TILE, TILE)]
            result[spot] = (total[spot] + got.astype(F32)).astype(BF16)
            out_copy(direction, tile).start()

    loads[0].wait()
    ring_step(0, False)
    pl.semaphore_wait(barrier, Z - 1 + 5)

    for direction, tile in ways:
        ring_copy(direction, 0, tile).start()
    gather_0(0)
    ring_step(1, True)
    own_base()
    for load in loads[1:]:
        load.wait()
    matches = [match(b) for b in range(blocks)]
    gather_1(0)
    ring_step(2, True)
    gather_2(0)
    gather_0(1)
    ring_step(3, True)
    gather_3(0)
    gather_1(1)
    ring_step(4, True)
    gather_4(0)
    gather_2(1)
    gather_5(0)
    ring_step(5, True)
    gather_6(0)
    shrink_parts(matches)
    gather_3(1)
    ring_step(6, True)
    shrink_sum()
    gather_4(1)
    gather_5(1)
    add_short()
    gather_6(1)
    expand(matches)
    finish()

    for slot in range(len(SLOTS)):
        for direction, tile in ways:
            ring_copy(direction, slot, tile).wait_send()
    for g in range(2):
        for kind in range(8):
            for j, direction in both:
                gather_copy(g, j, kind, direction).wait_send()
        for number in range(4):
            for j in range(2):
                across_copy(g, j, number).wait_send()
    for i in range(1, Z):
        part_copy(i).wait_send()
        shrunk_copy(i).wait_send()
    for direction, tile in ways:
        out_copy(direction, tile).wait()


def shards(acts, weight, block_ids, cached_a, cached_b, renewed_module_numbers, fresh_a, renewed_second_matrices):
    rows, depth = acts.shape
    width = cached_b.shape[2]
    blocks, rank = cached_b.shape[0], cached_b.shape[1]
    tiles = rows // 2 // TILE
    slots = len(SLOTS)
    dma = pltpu.SemaphoreType.DMA
    return pl.pallas_call(
        kernel,
        out_shape=jax.ShapeDtypeStruct((rows, width), BF16),
        in_specs=[pl.BlockSpec(memory_space=pl.ANY)] * 8,
        out_specs=pl.BlockSpec(memory_space=pl.ANY),
        scratch_shapes=[
            pltpu.VMEM((rows, depth), BF16),
            pltpu.VMEM((Z, depth, width), BF16),
            pltpu.SMEM(block_ids.shape, jnp.int32),
            pltpu.SMEM(renewed_module_numbers.shape, jnp.int32),
            pltpu.VMEM((blocks, rank, depth), BF16),
            pltpu.VMEM((blocks, rank, width), BF16),
            pltpu.VMEM((2 * 2 * SIDE * SIDE, rank, depth), BF16),
            pltpu.VMEM((2 * 2 * SIDE * SIDE, rank, width), BF16),
            pltpu.VMEM((2, slots, rows // 2, width), BF16),
            pltpu.VMEM((2, slots, rows // 2, width), BF16),
            pltpu.VMEM((rows, width), F32),
            pltpu.VMEM((rows, width), BF16),
            pltpu.VMEM((Z, rows // Z // 2, 2 * rank), BF16),
            pltpu.VMEM((Z, rows // Z // 2, 2 * rank), BF16),
            pltpu.VMEM((Z, rows // Z // 2, 2 * rank), BF16),
            dma((5,)),
            dma((Z,)),
            dma((2, 2)),
            dma((2, tiles)),
            dma((2, slots, tiles)),
            dma((2, slots, tiles)),
            dma((2, 2, 20)),
            dma((2, 2, 20)),
            dma((Z,)),
            dma((Z,)),
            dma((Z,)),
            dma((Z,)),
        ],
        compiler_params=pltpu.CompilerParams(
            collective_id=0, has_side_effects=True, vmem_limit_bytes=60 * 1024 * 1024
        ),
    )(
        acts, weight, block_ids, jnp.swapaxes(cached_a, 1, 2), cached_b,
        renewed_module_numbers, jnp.swapaxes(fresh_a, 1, 2), renewed_second_matrices,
    )


def solution(mesh):
    return jax.shard_map(
        shards,
        mesh=mesh,
        in_specs=(
            P("dp", "tensor"),
            P("tensor", None),
            P("dp"),
            P("dp", "tensor", None),
            P("dp", None, "tensor"),
            P(),
            P("dp", "tensor", None),
            P("dp", None, "tensor"),
        ),
        out_specs=P("dp", "tensor"),
        check_vma=False,
    )
```

time: 325 us -> 68.6 us (0.21)
  waiting for transfers between devices: 271 us -> 0 us
  Pallas kernels: 0 us -> 65.9 us
  matrix products: 36.5 us -> 0 us
  between operations: 13.1 us -> 0.01 us
    reduce_scatter x1 -> x0, waiting for transfers between devices: 113 us -> none  [shards(): lax.psum_scatter(base_product_sum, 'tensor', scatter_dimension=1, tiled=T...]
    all_gather x2 -> x0, waiting for transfers between devices: 89.4 us -> none  [the longest x1 61.9 us: shards(): lax.all_gather(fresh_a, 'dp', axis=0, tiled=True)]
    psum x1 -> x0, waiting for transfers between devices: 66.6 us -> none  [shards(): shrink = lax.psum(partial_value, 'tensor')]
    pallas_call x0 -> x1, Pallas kernels: none -> 65.9 us  [shards(): pl.pallas_call(kernel, out_shape=jax.ShapeDtypeStruct((rows, width), BF16...]
    dot_general x6 -> x0, matrix products: 36.5 us -> none  [the longest x1 12.3 us: shards(): jnp.einsum('bj,jik->bik', module_picker_matrix, every_a, preferred_elemen...]
  transfers between devices with their start and end apart: 4 -> 0, of which waited for: 4 -> 0; matrix products, arithmetic and copies ran while one was open for 12% -> 0% of each run, Pallas kernels for 0% -> 0%
where the time goes in v1:
time: 68.6 us; the launch traced here: 67.9 us
  Pallas kernels  65.9 us (96%)
  local copies, waits for them, and re-layouts  1.98 us (3%)
    pallas_call x1, Pallas kernels, shards(): pl.pallas_call(kernel, out_shape=jax.ShapeDtypeStruct((rows, width), BF16...  65.9 us
    unnamed x1, local copies, waits for them, and re-layouts  1.98 us

profile of v1, /device:TPU:4, one launch (start us, length us, event | category | flops | bytes accessed | tf_op | source)
XLA Modules:
  0.0 67.9 jit_solution(15847028358457886206)
XLA Ops:
  0.0 65.9 %shard_map.82 = bf16[512,640]{1,0:T(8,128)(2,1)} custom-call(bf16[512,1024]{1,0:T(8,128)(2,1)} %acts_hbm.1, bf16[1024,5120]{1,0:T(8,128)(2,1)} %weight_hbm.1, s32[4]{0:T(128)} %ids_hbm.1, bf16[4,64,1024]{2,1,0:T(8,128)(2,1)} %bitcast.2, bf16[4,64,640]{2,1,0:T(8,128)(2,1)} %cached_b_hbm.1, s32[64]{0:T(128)} %renewed_hbm.1, bf16[2,64,1024]{2,1,0:T(8,128)(2,1)} %bitcast.3, ...), custom_call_target="tpu_custom_call" | custom-call | tf_op jit(solution)/shard_map/pallas_call | solution.py:395
  65.9 2.0 %copy.10 = bf16[512,640]{1,0:T(8,128)(2,1)} copy(bf16[512,640]{1,0:T(8,128)(2,1)} %shard_map.82) | data formatting | bytes 1310720

commit v2 on v1

--- a/solution.py
+++ b/solution.py
@@ -33,10 +33,10 @@
 
 def kernel(
     acts_hbm, weight_hbm, ids_hbm, cached_a_hbm, cached_b_hbm, renewed_hbm, fresh_a_hbm, fresh_b_hbm,
-    out_hbm,
+    result,
     acts, weight, ids, renewed, cached_a, cached_b, every_a, every_b,
-    outgoing, incoming, total, result, part_out, part_in, shrunk,
-    load_sem, weight_sem, fresh_sem, out_sem,
+    outgoing, incoming, total, part_out, part_in, shrunk,
+    load_sem, weight_sem, fresh_sem,
     ring_send, ring_recv, gather_send, gather_recv, part_send, part_recv, shrunk_send, shrunk_recv,
 ):
     z = lax.axis_index("tensor")
@@ -222,11 +222,11 @@
     def gather_2(g):
         take_all(g, FIRST_FAR)
         send_all(g, SECOND_FAR)
-        send_across(g, 0)
-
-    def gather_3(g):
         take_all(g, SECOND)
         send_all(g, OWN_ON)
+        send_across(g, 0)
+
+    def gather_3(g):
         take_all(g, SECOND_PAIR)
         send_all(g, PAIR_ON)
 
@@ -320,17 +320,12 @@
             spot = lines(direction, False, tile)
             total[spot] = total[spot] + incoming[direction, LAST_SHORT, pl.ds(tile * TILE, TILE)].astype(F32)
 
-    def out_copy(direction, tile):
-        spot = lines(direction, True, tile)
-        return pltpu.make_async_copy(result.at[spot], out_hbm.at[spot], out_sem.at[direction, tile])
-
     def finish():
         for direction, tile in ways:
             ring_copy(direction, LAST_LONG, tile).wait_recv()
             spot = lines(direction, True, tile)
             got = incoming[direction, LAST_LONG, pl.ds(tile * TILE, TILE)]
             result[spot] = (total[spot] + got.astype(F32)).astype(BF16)
-            out_copy(direction, tile).start()
 
     loads[0].wait()
     ring_step(0, False)
@@ -347,24 +342,24 @@
     gather_1(0)
     ring_step(2, True)
     gather_2(0)
+    gather_3(0)
+    ring_step(3, True)
+    gather_4(0)
     gather_0(1)
-    ring_step(3, True)
-    gather_3(0)
+    ring_step(4, True)
+    gather_5(0)
     gather_1(1)
-    ring_step(4, True)
-    gather_4(0)
-    gather_2(1)
-    gather_5(0)
-    ring_step(5, True)
     gather_6(0)
     shrink_parts(matches)
+    gather_2(1)
+    ring_step(5, True)
     gather_3(1)
+    gather_4(1)
+    shrink_sum()
     ring_step(6, True)
-    shrink_sum()
-    gather_4(1)
     gather_5(1)
+    gather_6(1)
     add_short()
-    gather_6(1)
     expand(matches)
     finish()
 
@@ -381,8 +376,6 @@
     for i in range(1, Z):
         part_copy(i).wait_send()
         shrunk_copy(i).wait_send()
-    for direction, tile in ways:
-        out_copy(direction, tile).wait()
 
 
 def shards(acts, weight, block_ids, cached_a, cached_b, renewed_module_numbers, fresh_a, renewed_second_matrices):
@@ -394,9 +387,9 @@
     dma = pltpu.SemaphoreType.DMA
     return pl.pallas_call(
         kernel,
-        out_shape=jax.ShapeDtypeStruct((rows, width), BF16),
+        out_shape=pltpu.VMEM((rows, width), BF16),
         in_specs=[pl.BlockSpec(memory_space=pl.ANY)] * 8,
-        out_specs=pl.BlockSpec(memory_space=pl.ANY),
+        out_specs=pl.BlockSpec(memory_space=pltpu.VMEM),
         scratch_shapes=[
             pltpu.VMEM((rows, depth), BF16),
             pltpu.VMEM((Z, depth, width), BF16),
@@ -409,14 +402,12 @@
             pltpu.VMEM((2, slots, rows // 2, width), BF16),
             pltpu.VMEM((2, slots, rows // 2, width), BF16),
             pltpu.VMEM((rows, width), F32),
-            pltpu.VMEM((rows, width), BF16),
             pltpu.VMEM((Z, rows // Z // 2, 2 * rank), BF16),
             pltpu.VMEM((Z, rows // Z // 2, 2 * rank), BF16),
             pltpu.VMEM((Z, rows // Z // 2, 2 * rank), BF16),
             dma((5,)),
             dma((Z,)),
             dma((2, 2)),
-            dma((2, tiles)),
             dma((2, slots, tiles)),
             dma((2, slots, tiles)),
             dma((2, 2, 20)),

time: 68.6 us -> 64.8 us (0.945)
  Pallas kernels: 65.9 us -> 63.9 us
  local copies, waits for them, and re-layouts: 1.98 us -> 0.84 us
    pallas_call x1, Pallas kernels: 65.9 us -> 63.9 us  [shards(): pl.pallas_call(kernel, out_shape=pltpu.VMEM((rows, width), BF16), in_spec...]
    unnamed x1, local copies, waits for them, and re-layouts: 1.98 us -> 0.84 us
where the time goes in v2:
time: 64.8 us; the launch traced here: 64.7 us
  Pallas kernels  63.9 us (99%)
  local copies, waits for them, and re-layouts  0.84 us (1%)
    pallas_call x1, Pallas kernels, shards(): pl.pallas_call(kernel, out_shape=pltpu.VMEM((rows, width), BF16), in_spec...  63.9 us

profile of v2, /device:TPU:4, one launch (start us, length us, event | category | flops | bytes accessed | tf_op | source)
XLA Modules:
  0.0 64.7 jit_solution(9637848379978459431)
XLA Ops:
  0.0 63.9 %shard_map.82 = bf16[512,640]{1,0:T(8,128)(2,1)S(1)} custom-call(bf16[512,1024]{1,0:T(8,128)(2,1)} %acts_hbm.1, bf16[1024,5120]{1,0:T(8,128)(2,1)} %weight_hbm.1, s32[4]{0:T(128)} %ids_hbm.1, bf16[4,64,1024]{2,1,0:T(8,128)(2,1)} %bitcast.2, bf16[4,64,640]{2,1,0:T(8,128)(2,1)} %cached_b_hbm.1, s32[64]{0:T(128)} %renewed_hbm.1, bf16[2,64,1024]{2,1,0:T(8,128)(2,1)} %bitcast.3, ...), custom_call_target="tpu_custom_call" | custom-call | tf_op jit(solution)/shard_map/pallas_call | solution.py:388
  63.9 0.8 %copy.10 = bf16[512,640]{1,0:T(8,128)(2,1)} copy(bf16[512,640]{1,0:T(8,128)(2,1)S(1)} %shard_map.82) | data formatting | bytes 1310720

commit v3 on v2

--- a/solution.py
+++ b/solution.py
@@ -9,6 +9,7 @@
 Z = 8
 SIDE = 4
 TILE = 128
+PARTS = 2
 BF16 = jnp.bfloat16
 F32 = jnp.float32
 
@@ -35,7 +36,7 @@
     acts_hbm, weight_hbm, ids_hbm, cached_a_hbm, cached_b_hbm, renewed_hbm, fresh_a_hbm, fresh_b_hbm,
     result,
     acts, weight, ids, renewed, cached_a, cached_b, every_a, every_b,
-    outgoing, incoming, total, part_out, part_in, shrunk,
+    outgoing, incoming, total, part_out, part_in, merged, shrunk,
     load_sem, weight_sem, fresh_sem,
     ring_send, ring_recv, gather_send, gather_recv, part_send, part_recv, shrunk_send, shrunk_recv,
 ):
@@ -82,33 +83,26 @@
         for g, (held, source) in enumerate(gathers)
     ]
 
-    loads[0].start()
-    weight_load(4).start()
-
     barrier = pltpu.get_barrier_semaphore()
-    for i in range(1, Z):
+    for i in (1, Z - 1, 2, Z - 2, 3, Z - 3, 4):
         pl.semaphore_signal(barrier, inc=1, device_id={"tensor": (z + i) % Z}, device_id_type=pl.DeviceIdType.MESH)
     for axis in range(2):
         for step in (1, -1):
             pl.semaphore_signal(barrier, inc=1, device_id=along(axis, step), device_id_type=pl.DeviceIdType.MESH)
     pl.semaphore_signal(barrier, inc=1, device_id=sibling, device_id_type=pl.DeviceIdType.MESH)
 
+    weight_load(4).start()
+    loads[0].start()
     for j in range(2):
         fresh_loads[0][j].start()
-    for i in (3, 5, 2, 6, 1, 7, 0):
-        weight_load(i).start()
-    for j in range(2):
-        fresh_loads[1][j].start()
-    for load in loads[1:]:
-        load.start()
-
-    def ring_copy(direction, slot, tile):
-        spot = pl.ds(tile * TILE, TILE)
+
+    def ring_copy(direction, slot, tile, part=0, parts=1):
+        spot = pl.ds(tile * TILE + part * (TILE // parts), TILE // parts)
         return pltpu.make_async_remote_copy(
             src_ref=outgoing.at[direction, slot, spot],
             dst_ref=incoming.at[direction, slot, spot],
-            send_sem=ring_send.at[direction, slot, tile],
-            recv_sem=ring_recv.at[direction, slot, tile],
+            send_sem=ring_send.at[direction, slot, tile * PARTS + part],
+            recv_sem=ring_recv.at[direction, slot, tile * PARTS + part],
             device_id={"tensor": (z + 1 - 2 * direction + Z) % Z},
             device_id_type=pl.DeviceIdType.MESH,
         )
@@ -119,22 +113,37 @@
         side = direction if is_long else 1 - direction
         return pl.ds(side * half + tile * TILE, TILE)
 
-    def ring_step(slot, send):
+    def ring_piece(slot, direction, tile):
         is_long, step, before = SLOTS[slot]
-        if is_long and step == 0:
-            weight_load(4).wait()
-        elif not is_long:
+        spot = pl.ds(tile * TILE, TILE)
+        term = dot(acts[lines(direction, is_long, tile)], weight[4 - step + 2 * step * direction])
+        if before is not None:
+            ring_copy(direction, before, tile).wait_recv()
+            term = term + incoming[direction, before, spot].astype(F32)
+        outgoing[direction, slot, spot] = term.astype(BF16)
+
+    def ring_send_piece(slot, direction, tile):
+        parts = PARTS if slot == LAST_LONG else 1
+        for part in range(parts):
+            ring_copy(direction, slot, tile, part, parts).start()
+
+    def ring_step(slot):
+        is_long, step, _ = SLOTS[slot]
+        if not is_long:
             weight_load(4 - step).wait()
             weight_load(4 + step).wait()
-        for direction, tile in ways:
-            spot = pl.ds(tile * TILE, TILE)
-            term = dot(acts[lines(direction, is_long, tile)], weight[4 - step + 2 * step * direction])
-            if before is not None:
-                ring_copy(direction, before, tile).wait_recv()
-                term = term + incoming[direction, before, spot].astype(F32)
-            outgoing[direction, slot, spot] = term.astype(BF16)
+        for tile in range(tiles):
+            ring_tile(slot, tile)
+
+    def ring_tile(slot, tile, send=True):
+        for direction in range(2):
+            ring_piece(slot, direction, tile)
             if send:
-                ring_copy(direction, slot, tile).start()
+                ring_send_piece(slot, direction, tile)
+
+    def ring_out(slot, tile):
+        for direction in range(2):
+            ring_send_piece(slot, direction, tile)
 
     def line_of(j, second, of_core):
         return ((j * 2 + of_core) * SIDE + second) * SIDE
@@ -259,18 +268,43 @@
 
     piece = rows // Z
 
-    def part_copy(i):
+    slice_half = piece // 4
+    ADJACENT, THIRD, FOURTH, MERGED = range(4)
+
+    def toward(direction, distance):
+        return (z + distance * (1 - 2 * direction) + Z) % Z
+
+    def half_of(direction):
+        return pl.ds(direction * slice_half, slice_half)
+
+    def part_copy(kind, direction):
+        if kind == ADJACENT:
+            src, distance = part_out.at[toward(direction, 1)], 1
+        elif kind == THIRD:
+            src, distance = part_out.at[toward(direction, 3)], 1
+        elif kind == FOURTH:
+            src, distance = part_out.at[toward(direction, 4), half_of(direction)], 2
+        else:
+            src, distance = merged.at[direction], 2
+        dst = part_in.at[kind, direction]
         return pltpu.make_async_remote_copy(
-            src_ref=part_out.at[(z + i) % Z], dst_ref=part_in.at[i],
-            send_sem=part_send.at[i], recv_sem=part_recv.at[i],
-            device_id={"tensor": (z + i) % Z}, device_id_type=pl.DeviceIdType.MESH,
+            src_ref=src, dst_ref=dst.at[half_of(direction)] if kind == FOURTH else dst,
+            send_sem=part_send.at[kind, direction], recv_sem=part_recv.at[kind, direction],
+            device_id={"tensor": toward(direction, distance)}, device_id_type=pl.DeviceIdType.MESH,
         )
 
-    def shrunk_copy(i):
+    def shrunk_copy(kind, direction):
+        if kind < 2:
+            src, dst, distance = shrunk.at[0], shrunk.at[(Z - 1 - kind) if direction else 1 + kind], 1 + kind
+        elif kind == 2:
+            src, dst, distance = shrunk.at[6 if direction else 2], shrunk.at[5 if direction else 3], 1
+        else:
+            spot = half_of(direction)
+            src, dst, distance = shrunk.at[6 if direction else 2, spot], shrunk.at[4, spot], 2
         return pltpu.make_async_remote_copy(
-            src_ref=shrunk.at[0], dst_ref=shrunk.at[i],
-            send_sem=shrunk_send.at[i], recv_sem=shrunk_recv.at[i],
-            device_id={"tensor": (z + i) % Z}, device_id_type=pl.DeviceIdType.MESH,
+            src_ref=src, dst_ref=dst,
+            send_sem=shrunk_send.at[kind, direction], recv_sem=shrunk_recv.at[kind, direction],
+            device_id={"tensor": toward(direction, distance)}, device_id_type=pl.DeviceIdType.MESH,
         )
 
     def shrink_parts(matches):
@@ -283,21 +317,43 @@
                 upper = part[q * piece : q * piece + piece // 2]
                 lower = part[q * piece + piece // 2 : (q + 1) * piece]
                 part_out[b * (TILE // piece) + q] = jnp.concatenate([upper, lower], axis=1).astype(BF16)
-        for i in range(1, Z):
-            part_copy(i).start()
+        for kind in (THIRD, FOURTH, ADJACENT):
+            for direction in range(2):
+                part_copy(kind, direction).start()
+
+    def shrink_merge():
+        for direction in range(2):
+            part_copy(THIRD, direction).wait_recv()
+            part_copy(FOURTH, direction).wait_recv()
+            value = part_out[toward(direction, 2)].astype(F32) + part_in[THIRD, direction].astype(F32)
+            spot = half_of(direction)
+            rest = half_of(1 - direction)
+            share = value[direction * slice_half : (direction + 1) * slice_half]
+            merged[direction, spot] = (share + part_in[FOURTH, direction, spot].astype(F32)).astype(BF16)
+            merged[direction, rest] = value[(1 - direction) * slice_half : (2 - direction) * slice_half].astype(BF16)
+            part_copy(MERGED, direction).start()
 
     def shrink_sum():
         value = part_out[z].astype(F32)
-        for i in range(1, Z):
-            part_copy(i).wait_recv()
-            value = value + part_in[i].astype(F32)
+        for kind in (ADJACENT, MERGED):
+            for direction in range(2):
+                part_copy(kind, direction).wait_recv()
+                value = value + part_in[kind, direction].astype(F32)
         shrunk[0] = value.astype(BF16)
-        for i in range(1, Z):
-            shrunk_copy(i).start()
+        for kind in (1, 0):
+            for direction in range(2):
+                shrunk_copy(kind, direction).start()
+
+    def shrink_relay():
+        for direction in range(2):
+            shrunk_copy(1, direction).wait_recv()
+            shrunk_copy(3, direction).start()
+            shrunk_copy(2, direction).start()
 
     def expand(matches):
-        for i in range(1, Z):
-            shrunk_copy(i).wait_recv()
+        for kind in (0, 2, 3):
+            for direction in range(2):
+                shrunk_copy(kind, direction).wait_recv()
         for b in range(blocks):
             factor = chosen(every_b, cached_b, b, *matches[b])
             lines = []
@@ -321,61 +377,94 @@
             total[spot] = total[spot] + incoming[direction, LAST_SHORT, pl.ds(tile * TILE, TILE)].astype(F32)
 
     def finish():
-        for direction, tile in ways:
-            ring_copy(direction, LAST_LONG, tile).wait_recv()
-            spot = lines(direction, True, tile)
-            got = incoming[direction, LAST_LONG, pl.ds(tile * TILE, TILE)]
-            result[spot] = (total[spot] + got.astype(F32)).astype(BF16)
-
-    loads[0].wait()
-    ring_step(0, False)
-    pl.semaphore_wait(barrier, Z - 1 + 5)
-
-    for direction, tile in ways:
-        ring_copy(direction, 0, tile).start()
-    gather_0(0)
-    ring_step(1, True)
-    own_base()
-    for load in loads[1:]:
-        load.wait()
-    matches = [match(b) for b in range(blocks)]
-    gather_1(0)
-    ring_step(2, True)
-    gather_2(0)
-    gather_3(0)
-    ring_step(3, True)
-    gather_4(0)
-    gather_0(1)
-    ring_step(4, True)
-    gather_5(0)
-    gather_1(1)
-    gather_6(0)
-    shrink_parts(matches)
-    gather_2(1)
-    ring_step(5, True)
-    gather_3(1)
-    gather_4(1)
-    shrink_sum()
-    ring_step(6, True)
-    gather_5(1)
-    gather_6(1)
-    add_short()
-    expand(matches)
-    finish()
-
-    for slot in range(len(SLOTS)):
-        for direction, tile in ways:
-            ring_copy(direction, slot, tile).wait_send()
-    for g in range(2):
+        size = TILE // PARTS
+        for tile in range(tiles):
+            for part in range(PARTS):
+                for direction in range(2):
+                    ring_copy(direction, LAST_LONG, tile, part, PARTS).wait_recv()
+                    side = direction * half
+                    spot = pl.ds(side + tile * TILE + part * size, size)
+                    got = incoming[direction, LAST_LONG, pl.ds(tile * TILE + part * size, size)]
+                    result[spot] = (total[spot] + got.astype(F32)).astype(BF16)
+
+    def drain_gather(g):
         for kind in range(8):
             for j, direction in both:
                 gather_copy(g, j, kind, direction).wait_send()
         for number in range(4):
             for j in range(2):
                 across_copy(g, j, number).wait_send()
-    for i in range(1, Z):
-        part_copy(i).wait_send()
-        shrunk_copy(i).wait_send()
+
+    def drain_ring(*slots):
+        for slot in slots:
+            parts = PARTS if slot == LAST_LONG else 1
+            for direction, tile in ways:
+                for part in range(parts):
+                    ring_copy(direction, slot, tile, part, parts).wait_send()
+
+    weight_load(4).wait()
+    loads[0].wait()
+    for direction in range(2):
+        ring_piece(0, direction, 0)
+    pl.semaphore_wait(barrier, Z - 1 + 5)
+    for direction in range(2):
+        ring_send_piece(0, direction, 0)
+    for direction in range(2):
+        for tile in range(1, tiles):
+            ring_piece(0, direction, tile)
+            ring_send_piece(0, direction, tile)
+    gather_0(0)
+    for i in (3, 5, 2, 6, 1, 7, 0):
+        weight_load(i).start()
+    for j in range(2):
+        fresh_loads[1][j].start()
+    for load in loads[1:]:
+        load.start()
+    ring_step(1)
+    own_base()
+    for load in loads[1:]:
+        load.wait()
+    matches = [match(b) for b in range(blocks)]
+    gather_1(0)
+    ring_step(2)
+    gather_2(0)
+    gather_3(0)
+    ring_step(3)
+    gather_4(0)
+    gather_0(1)
+    ring_step(4)
+    gather_5(0)
+    gather_1(1)
+    gather_6(0)
+    shrink_parts(matches)
+    gather_2(1)
+    weight_load(1).wait()
+    weight_load(7).wait()
+    ring_tile(5, 0)
+    ring_tile(5, 1, False)
+    shrink_merge()
+    ring_out(5, 1)
+    gather_3(1)
+    gather_4(1)
+    ring_tile(6, 0, False)
+    shrink_sum()
+    ring_out(6, 0)
+    ring_tile(6, 1, False)
+    gather_5(1)
+    shrink_relay()
+    ring_out(6, 1)
+    gather_6(1)
+    add_short()
+    drain_gather(0)
+    drain_gather(1)
+    drain_ring(0, 1, 2, 3, 4, 5)
+    expand(matches)
+    for kind in range(4):
+        for direction in range(2):
+            part_copy(kind, direction).wait_send()
+            shrunk_copy(kind, direction).wait_send()
+    finish()
+    drain_ring(6)
 
 
 def shards(acts, weight, block_ids, cached_a, cached_b, renewed_module_numbers, fresh_a, renewed_second_matrices):
@@ -403,19 +492,20 @@
             pltpu.VMEM((2, slots, rows // 2, width), BF16),
             pltpu.VMEM((rows, width), F32),
             pltpu.VMEM((Z, rows // Z // 2, 2 * rank), BF16),
-            pltpu.VMEM((Z, rows // Z // 2, 2 * rank), BF16),
+            pltpu.VMEM((4, 2, rows // Z // 2, 2 * rank), BF16),
+            pltpu.VMEM((2, rows // Z // 2, 2 * rank), BF16),
             pltpu.VMEM((Z, rows // Z // 2, 2 * rank), BF16),
             dma((5,)),
             dma((Z,)),
             dma((2, 2)),
-            dma((2, slots, tiles)),
-            dma((2, slots, tiles)),
+            dma((2, slots, tiles * PARTS)),
+            dma((2, slots, tiles * PARTS)),
             dma((2, 2, 20)),
             dma((2, 2, 20)),
-            dma((Z,)),
-            dma((Z,)),
-            dma((Z,)),
-            dma((Z,)),
+            dma((4, 2)),
+            dma((4, 2)),
+            dma((4, 2)),
+            dma((4, 2)),
         ],
         compiler_params=pltpu.CompilerParams(
             collective_id=0, has_side_effects=True, vmem_limit_bytes=60 * 1024 * 1024

time: 64.8 us -> 64.1 us (0.989)
  Pallas kernels: 63.9 us -> 63.1 us
    pallas_call x1, Pallas kernels: 63.9 us -> 63.1 us  [shards(): pl.pallas_call(kernel, out_shape=pltpu.VMEM((rows, width), BF16), in_spec...]
where the time goes in v3:
time: 64.1 us; the launch traced here: 64 us
  Pallas kernels  63.1 us (98%)
  local copies, waits for them, and re-layouts  0.84 us (1%)
    pallas_call x1, Pallas kernels, shards(): pl.pallas_call(kernel, out_shape=pltpu.VMEM((rows, width), BF16), in_spec...  63.1 us

profile of v3, /device:TPU:4, one launch (start us, length us, event | category | flops | bytes accessed | tf_op | source)
XLA Modules:
  0.0 64.0 jit_solution(9781390291156790435)
XLA Ops:
  0.0 63.1 %shard_map.82 = bf16[512,640]{1,0:T(8,128)(2,1)S(1)} custom-call(bf16[512,1024]{1,0:T(8,128)(2,1)} %acts_hbm.1, bf16[1024,5120]{1,0:T(8,128)(2,1)} %weight_hbm.1, s32[4]{0:T(128)} %ids_hbm.1, bf16[4,64,1024]{2,1,0:T(8,128)(2,1)} %bitcast.2, bf16[4,64,640]{2,1,0:T(8,128)(2,1)} %cached_b_hbm.1, s32[64]{0:T(128)} %renewed_hbm.1, bf16[2,64,1024]{2,1,0:T(8,128)(2,1)} %bitcast.3, ...), custom_call_target="tpu_custom_call" | custom-call | tf_op jit(solution)/shard_map/pallas_call | solution.py:477
  63.1 0.8 %copy.10 = bf16[512,640]{1,0:T(8,128)(2,1)} copy(bf16[512,640]{1,0:T(8,128)(2,1)S(1)} %shard_map.82) | data formatting | bytes 1310720

commit v4 on v3

--- a/solution.py
+++ b/solution.py
@@ -10,6 +10,7 @@
 SIDE = 4
 TILE = 128
 PARTS = 2
+SHIFTED = (7, 4)
 BF16 = jnp.bfloat16
 F32 = jnp.float32
 
@@ -36,9 +37,9 @@
     acts_hbm, weight_hbm, ids_hbm, cached_a_hbm, cached_b_hbm, renewed_hbm, fresh_a_hbm, fresh_b_hbm,
     result,
     acts, weight, ids, renewed, cached_a, cached_b, every_a, every_b,
-    outgoing, incoming, total, part_out, part_in, merged, shrunk,
+    outgoing, incoming, strip_in, total, part_out, part_in, merged, shrunk,
     load_sem, weight_sem, fresh_sem,
-    ring_send, ring_recv, gather_send, gather_recv, part_send, part_recv, shrunk_send, shrunk_recv,
+    ring_send, ring_recv, strip_send, strip_recv, gather_send, gather_recv, part_send, part_recv, shrunk_send, shrunk_recv,
 ):
     z = lax.axis_index("tensor")
     dp = lax.axis_index("dp")
@@ -84,7 +85,7 @@
     ]
 
     barrier = pltpu.get_barrier_semaphore()
-    for i in (1, Z - 1, 2, Z - 2, 3, Z - 3, 4):
+    for i in (1, Z - 1):
         pl.semaphore_signal(barrier, inc=1, device_id={"tensor": (z + i) % Z}, device_id_type=pl.DeviceIdType.MESH)
     for axis in range(2):
         for step in (1, -1):
@@ -113,19 +114,77 @@
         side = direction if is_long else 1 - direction
         return pl.ds(side * half + tile * TILE, TILE)
 
+    strip = pl.ds(half - TILE // PARTS, TILE // PARTS)
+
+    def parts_of(slot, tile):
+        return PARTS if slot == LAST_LONG or (slot < 2 and tile == tiles - 1) else 1
+
+    def copies_of(slot, direction, tile):
+        parts = parts_of(slot, tile)
+        return [ring_copy(direction, slot, tile, part, parts) for part in range(parts)]
+
+    def strip_other(direction):
+        return pltpu.make_async_remote_copy(
+            src_ref=outgoing.at[1 - direction, 0, strip],
+            dst_ref=strip_in.at[direction],
+            send_sem=strip_send.at[direction],
+            recv_sem=strip_recv.at[direction],
+            device_id={"tensor": (z + 1 - 2 * direction + Z) % Z},
+            device_id_type=pl.DeviceIdType.MESH,
+        )
+
+    def before_me(direction):
+        return (z - 1 + 2 * direction + Z) % Z
+
     def ring_piece(slot, direction, tile):
         is_long, step, before = SLOTS[slot]
         spot = pl.ds(tile * TILE, TILE)
         term = dot(acts[lines(direction, is_long, tile)], weight[4 - step + 2 * step * direction])
+        if before == 0 and tile == tiles - 1:
+            first = pl.ds(tile * TILE, TILE // PARTS)
+            kept, ends = copies_of(0, direction, tile)
+            kept.wait_recv()
+            upper = term[: TILE // PARTS] + incoming[direction, 0, first].astype(F32)
+            outgoing[direction, slot, first] = upper.astype(BF16)
+            outgoing[direction, slot, strip] = term[TILE // PARTS :].astype(BF16)
+
+            @pl.when(before_me(direction) != SHIFTED[direction])
+            def _():
+                ends.wait_recv()
+                lower = outgoing[direction, slot, strip].astype(F32) + incoming[direction, 0, strip].astype(F32)
+                outgoing[direction, slot, strip] = lower.astype(BF16)
+
+            return
         if before is not None:
-            ring_copy(direction, before, tile).wait_recv()
+            for copy in copies_of(before, direction, tile):
+                copy.wait_recv()
             term = term + incoming[direction, before, spot].astype(F32)
         outgoing[direction, slot, spot] = term.astype(BF16)
 
     def ring_send_piece(slot, direction, tile):
-        parts = PARTS if slot == LAST_LONG else 1
-        for part in range(parts):
-            ring_copy(direction, slot, tile, part, parts).start()
+        copies = copies_of(slot, direction, tile)
+        if slot < 2 and tile == tiles - 1:
+            copies[0].start()
+            if slot == 0:
+                pl.when(z != SHIFTED[direction])(copies[1].start)
+            return
+        for copy in copies:
+            copy.start()
+
+    def strips_away():
+        for direction in range(2):
+            pl.when(z == SHIFTED[1 - direction])(strip_other(direction).start)
+
+    def strips_on():
+        for direction in range(2):
+
+            @pl.when(before_me(direction) == SHIFTED[1 - direction])
+            def _():
+                strip_other(direction).wait_recv()
+                value = outgoing[direction, 1, strip].astype(F32) + strip_in[direction].astype(F32)
+                outgoing[direction, 1, strip] = value.astype(BF16)
+
+            copies_of(1, direction, tiles - 1)[1].start()
 
     def ring_step(slot):
         is_long, step, _ = SLOTS[slot]
@@ -397,22 +456,28 @@
 
     def drain_ring(*slots):
         for slot in slots:
-            parts = PARTS if slot == LAST_LONG else 1
             for direction, tile in ways:
-                for part in range(parts):
-                    ring_copy(direction, slot, tile, part, parts).wait_send()
+                copies = copies_of(slot, direction, tile)
+                if slot == 0 and tile == tiles - 1:
+                    copies[0].wait_send()
+                    pl.when(z != SHIFTED[direction])(copies[1].wait_send)
+                    pl.when(z == SHIFTED[1 - direction])(strip_other(direction).wait_send)
+                    continue
+                for copy in copies:
+                    copy.wait_send()
 
     weight_load(4).wait()
     loads[0].wait()
     for direction in range(2):
         ring_piece(0, direction, 0)
-    pl.semaphore_wait(barrier, Z - 1 + 5)
+    pl.semaphore_wait(barrier, 7)
     for direction in range(2):
         ring_send_piece(0, direction, 0)
     for direction in range(2):
         for tile in range(1, tiles):
             ring_piece(0, direction, tile)
             ring_send_piece(0, direction, tile)
+    strips_away()
     gather_0(0)
     for i in (3, 5, 2, 6, 1, 7, 0):
         weight_load(i).start()
@@ -427,6 +492,7 @@
     matches = [match(b) for b in range(blocks)]
     gather_1(0)
     ring_step(2)
+    strips_on()
     gather_2(0)
     gather_3(0)
     ring_step(3)
@@ -490,6 +556,7 @@
             pltpu.VMEM((2 * 2 * SIDE * SIDE, rank, width), BF16),
             pltpu.VMEM((2, slots, rows // 2, width), BF16),
             pltpu.VMEM((2, slots, rows // 2, width), BF16),
+            pltpu.VMEM((2, TILE // PARTS, width), BF16),
             pltpu.VMEM((rows, width), F32),
             pltpu.VMEM((Z, rows // Z // 2, 2 * rank), BF16),
             pltpu.VMEM((4, 2, rows // Z // 2, 2 * rank), BF16),
@@ -500,6 +567,8 @@
             dma((2, 2)),
             dma((2, slots, tiles * PARTS)),
             dma((2, slots, tiles * PARTS)),
+            dma((2,)),
+            dma((2,)),
             dma((2, 2, 20)),
             dma((2, 2, 20)),
             dma((4, 2)),

time: 64.1 us -> 63.6 us (level)
  no operation moved by 1% of the time
where the time goes in v4:
time: 63.6 us; the launch traced here: 63.5 us
  Pallas kernels  62.7 us (99%)
  local copies, waits for them, and re-layouts  0.84 us (1%)
    pallas_call x1, Pallas kernels, shards(): pl.pallas_call(kernel, out_shape=pltpu.VMEM((rows, width), BF16), in_spec...  62.7 us

profile of v4, /device:TPU:4, one launch (start us, length us, event | category | flops | bytes accessed | tf_op | source)
XLA Modules:
  0.0 63.5 jit_solution(2367812701546097847)
XLA Ops:
  0.0 62.7 %shard_map.82 = bf16[512,640]{1,0:T(8,128)(2,1)S(1)} custom-call(bf16[512,1024]{1,0:T(8,128)(2,1)} %acts_hbm.1, bf16[1024,5120]{1,0:T(8,128)(2,1)} %weight_hbm.1, s32[4]{0:T(128)} %ids_hbm.1, bf16[4,64,1024]{2,1,0:T(8,128)(2,1)} %bitcast.2, bf16[4,64,640]{2,1,0:T(8,128)(2,1)} %cached_b_hbm.1, s32[64]{0:T(128)} %renewed_hbm.1, bf16[2,64,1024]{2,1,0:T(8,128)(2,1)} %bitcast.3, ...), custom_call_target="tpu_custom_call" | custom-call | tf_op jit(solution)/shard_map/pallas_call | solution.py:543
  62.7 0.8 %copy.10 = bf16[512,640]{1,0:T(8,128)(2,1)} copy(bf16[512,640]{1,0:T(8,128)(2,1)S(1)} %shard_map.82) | data formatting | bytes 1310720

commit v5 on v4

--- a/solution.py
+++ b/solution.py
@@ -516,9 +516,12 @@
     shrink_sum()
     ring_out(6, 0)
     ring_tile(6, 1, False)
+    for direction in range(2):
+        copies_of(6, direction, 1)[0].start()
     gather_5(1)
     shrink_relay()
-    ring_out(6, 1)
+    for direction in range(2):
+        copies_of(6, direction, 1)[1].start()
     gather_6(1)
     add_short()
     drain_gather(0)

time: 63.6 us -> 64.4 us (1.013)
  Pallas kernels: 62.7 us -> 63.4 us
    pallas_call x1, Pallas kernels: 62.7 us -> 63.4 us  [shards(): pl.pallas_call(kernel, out_shape=pltpu.VMEM((rows, width), BF16), in_spec...]
where the time goes in v5:
time: 64.4 us; the launch traced here: 64.3 us
  Pallas kernels  63.4 us (98%)
  local copies, waits for them, and re-layouts  0.84 us (1%)
    pallas_call x1, Pallas kernels, shards(): pl.pallas_call(kernel, out_shape=pltpu.VMEM((rows, width), BF16), in_spec...  63.4 us

profile of v5, /device:TPU:4, one launch (start us, length us, event | category | flops | bytes accessed | tf_op | source)
XLA Modules:
  0.0 64.3 jit_solution(2683222718697780060)
XLA Ops:
  0.0 63.4 %shard_map.82 = bf16[512,640]{1,0:T(8,128)(2,1)S(1)} custom-call(bf16[512,1024]{1,0:T(8,128)(2,1)} %acts_hbm.1, bf16[1024,5120]{1,0:T(8,128)(2,1)} %weight_hbm.1, s32[4]{0:T(128)} %ids_hbm.1, bf16[4,64,1024]{2,1,0:T(8,128)(2,1)} %bitcast.2, bf16[4,64,640]{2,1,0:T(8,128)(2,1)} %cached_b_hbm.1, s32[64]{0:T(128)} %renewed_hbm.1, bf16[2,64,1024]{2,1,0:T(8,128)(2,1)} %bitcast.3, ...), custom_call_target="tpu_custom_call" | custom-call | tf_op jit(solution)/shard_map/pallas_call | solution.py:546
  63.5 0.8 %copy.10 = bf16[512,640]{1,0:T(8,128)(2,1)} copy(bf16[512,640]{1,0:T(8,128)(2,1)S(1)} %shard_map.82) | data formatting | bytes 1310720

commit v6 on v4

--- a/solution.py
+++ b/solution.py
@@ -37,7 +37,7 @@
     acts_hbm, weight_hbm, ids_hbm, cached_a_hbm, cached_b_hbm, renewed_hbm, fresh_a_hbm, fresh_b_hbm,
     result,
     acts, weight, ids, renewed, cached_a, cached_b, every_a, every_b,
-    outgoing, incoming, strip_in, total, part_out, part_in, merged, shrunk,
+    outgoing, incoming, strip_in, total, part_out, part_in, merged, shrunk, factor_b,
     load_sem, weight_sem, fresh_sem,
     ring_send, ring_recv, strip_send, strip_recv, gather_send, gather_recv, part_send, part_recv, shrunk_send, shrunk_recv,
 ):
@@ -409,19 +409,22 @@
             shrunk_copy(3, direction).start()
             shrunk_copy(2, direction).start()
 
-    def expand(matches):
-        for kind in (0, 2, 3):
+    def choose_b(matches):
+        for b in range(blocks):
+            factor_b[b] = chosen(every_b, cached_b, b, *matches[b])
+
+    def expand(*slices):
+        for i in slices:
+            q = (z + Z - i) % Z
+            packed = shrunk[i].astype(F32)
+            lines = jnp.concatenate([packed[:, :rank], packed[:, rank:]], axis=0).astype(BF16)
+            spot = pl.ds(pl.multiple_of(q * piece, piece), piece)
+            total[spot] = total[spot] + adapter_scale * dot(lines, factor_b[q // (TILE // piece)])
+
+    def take_shrunk(*kinds):
+        for kind in kinds:
             for direction in range(2):
                 shrunk_copy(kind, direction).wait_recv()
-        for b in range(blocks):
-            factor = chosen(every_b, cached_b, b, *matches[b])
-            lines = []
-            for q in range(TILE // piece):
-                packed = shrunk[(z + Z - b * (TILE // piece) - q) % Z].astype(F32)
-                lines += [packed[:, :rank], packed[:, rank:]]
-            lines = jnp.concatenate(lines, axis=0).astype(BF16)
-            spot = pl.ds(b * TILE, TILE)
-            total[spot] = total[spot] + adapter_scale * dot(lines, factor)
 
     def own_base():
         weight_load(0).wait()
@@ -520,11 +523,15 @@
     shrink_relay()
     ring_out(6, 1)
     gather_6(1)
+    choose_b(matches)
+    take_shrunk(0)
+    expand(0, 1, 7, 2, 6)
     add_short()
     drain_gather(0)
     drain_gather(1)
     drain_ring(0, 1, 2, 3, 4, 5)
-    expand(matches)
+    take_shrunk(2, 3)
+    expand(3, 5, 4)
     for kind in range(4):
         for direction in range(2):
             part_copy(kind, direction).wait_send()
@@ -562,6 +569,7 @@
             pltpu.VMEM((4, 2, rows // Z // 2, 2 * rank), BF16),
             pltpu.VMEM((2, rows // Z // 2, 2 * rank), BF16),
             pltpu.VMEM((Z, rows // Z // 2, 2 * rank), BF16),
+            pltpu.VMEM((blocks, rank, width), BF16),
             dma((5,)),
             dma((Z,)),
             dma((2, 2)),

time: 63.6 us -> 63.6 us (level)
  no operation moved by 1% of the time
where the time goes in v6:
time: 63.6 us; the launch traced here: 63.5 us
  Pallas kernels  62.7 us (99%)
  local copies, waits for them, and re-layouts  0.84 us (1%)
    pallas_call x1, Pallas kernels, shards(): pl.pallas_call(kernel, out_shape=pltpu.VMEM((rows, width), BF16), in_spec...  62.7 us

profile of v6, /device:TPU:4, one launch (start us, length us, event | category | flops | bytes accessed | tf_op | source)
XLA Modules:
  0.0 63.5 jit_solution(16649034896582141697)
XLA Ops:
  0.0 62.7 %shard_map.82 = bf16[512,640]{1,0:T(8,128)(2,1)S(1)} custom-call(bf16[512,1024]{1,0:T(8,128)(2,1)} %acts_hbm.1, bf16[1024,5120]{1,0:T(8,128)(2,1)} %weight_hbm.1, s32[4]{0:T(128)} %ids_hbm.1, bf16[4,64,1024]{2,1,0:T(8,128)(2,1)} %bitcast.2, bf16[4,64,640]{2,1,0:T(8,128)(2,1)} %cached_b_hbm.1, s32[64]{0:T(128)} %renewed_hbm.1, bf16[2,64,1024]{2,1,0:T(8,128)(2,1)} %bitcast.3, ...), custom_call_target="tpu_custom_call" | custom-call | tf_op jit(solution)/shard_map/pallas_call | solution.py:550
  62.7 0.8 %copy.10 = bf16[512,640]{1,0:T(8,128)(2,1)} copy(bf16[512,640]{1,0:T(8,128)(2,1)S(1)} %shard_map.82) | data formatting | bytes 1310720
